TPU v7x, 512 devices: a whole 4x4x16 slice. The times are simulated.
512 devices in a mesh: leaf: 32 (over y_hi, z), grid: 16 (over x, y_lo, core).
Axes of the slice: x: 4, y: 4 (y_hi: 2, y_lo: 2; y = y_hi * 2 + y_lo), z: 16, core: 2. Of those that a mesh axis runs over, the one named last changes fastest.
Arguments:
- samples: bfloat16 [32, 512, 1024], P('leaf', 'grid'), may hold values from -6 to 6
- omega: bfloat16 [32, 512, 1024], P('leaf', 'grid'), may hold values from -6 to 6
- points: bfloat16 [8, 32, 512], P(None, 'leaf', 'grid'), may hold values from -5 to 5
- ranks: int32 [3, 32], replicated, may hold values from 256 to 512, as said below
- pivots: int32 [2, 32, 512], P(None, 'leaf'), may hold values from 0 to 1023, as said below
Outputs:
- top_samples: bfloat16 [32, 512, 1024], P('leaf', 'grid')
Inputs may be any that keep to these rules, and one draw needn't show every extreme that they name: `ranks`: equal for all groups under one node. At every level, some node has rank 512 and some node has rank half of 512. `pivots`: rows of the two stacked children (below 512: first child; 512 and up: second child); within one list distinct, and each below its child's rank; equal for all groups under one parent.
All inputs are finite; a program needn't handle non-finite values.
Results may differ from a plain program's by a relative error of at most 0.0038.
Values may be sent and summed in bfloat16 or wider, within the bound.
A program may use at most 64 MiB of HBM per device.

v0:
```python
import jax
import jax.numpy as jnp
from jax import lax
from jax.sharding import PartitionSpec as P

kernel_rate = 0.6
ridge_shift = 1.0


def from_partner(x, axis, bit):
    return lax.ppermute(x, axis, [(i, i ^ 1 << bit) for i in range(lax.axis_size(axis))])


def kernel_block(left, right, left_ids):
    distance = jnp.zeros((left.shape[1], right.shape[1]), jnp.float32)
    for component in range(left.shape[0]):
        spread = (
            left[component].astype(jnp.float32)[:, None]
            - right[component].astype(jnp.float32)[None, :]
        )
        distance = distance + spread * spread
    column_ids = jnp.arange(right.shape[1], dtype=jnp.int32)
    diagonal = (left_ids[:, None] == column_ids[None, :]).astype(jnp.float32)
    return (jnp.exp(-kernel_rate * distance) + ridge_shift * diagonal).astype(jnp.bfloat16)


def keep_alive(values, rank_now, row_ids):
    return jnp.where((row_ids < rank_now)[:, None], values, jnp.zeros_like(values))


def order_pair(parity, mine, sibling):
    leading = jnp.where(parity, sibling, mine)
    trailing = jnp.where(parity, mine, sibling)
    return (leading, trailing)


def body(samples, omega, points, ranks, pivots):
    grid_count = lax.axis_size("grid")
    leaf_pos = lax.axis_index("leaf")
    grid_pos = lax.axis_index("grid")
    local_rows = samples.shape[1]
    full_rank = local_rows * grid_count
    height_total = pivots.shape[0]
    coords = lax.all_gather(points, "grid", axis=2, tiled=True)[:, 0, :]
    first_rank = lax.dynamic_index_in_dim(ranks[0], leaf_pos, 0, keepdims=False)
    local_ids = grid_pos * local_rows + jnp.arange(local_rows, dtype=jnp.int32)
    mine_ids = jnp.concatenate([local_ids, full_rank + local_ids])
    columns = samples.shape[2]
    current_samples = keep_alive(samples[0], first_rank, local_ids)
    current_omega = keep_alive(omega[0], first_rank, local_ids)
    for height in range(height_total):
        sibling = from_partner((current_samples, current_omega, coords), "leaf", height)
        parity = leaf_pos >> height & 1 == 1
        lead_samples, trail_samples = order_pair(parity, current_samples, sibling[0])
        lead_omega, trail_omega = order_pair(parity, current_omega, sibling[1])
        lead_coords, trail_coords = order_pair(parity, coords, sibling[2])
        stacked_samples = jnp.stack([lead_samples, trail_samples])
        stacked_omega = jnp.stack([lead_omega, trail_omega])
        stacked_coords = jnp.concatenate([lead_coords, trail_coords], 1)
        block = kernel_block(jnp.take(stacked_coords, mine_ids, axis=1), stacked_coords, mine_ids)
        chosen = lax.dynamic_slice_in_dim(pivots[height, 0], grid_pos * local_rows, local_rows)

        def pick_rows(incoming):
            targets = jnp.arange(incoming.shape[1], dtype=jnp.int32)
            lead_pick = (chosen[:, None] == targets[None, :]).astype(jnp.bfloat16)
            trail_pick = (chosen[:, None] == full_rank + targets[None, :]).astype(jnp.bfloat16)
            return jnp.dot(lead_pick, incoming[0], preferred_element_type=jnp.float32) + jnp.dot(
                trail_pick, incoming[1], preferred_element_type=jnp.float32
            )

        apply_incoming = lax.all_gather(stacked_omega, "grid", axis=1, tiled=True)
        width_now = apply_incoming.shape[1]
        lead_cols = lax.slice_in_dim(block, 0, width_now, axis=1)
        trail_cols = lax.dynamic_slice_in_dim(block, full_rank, width_now, 1)
        product = jnp.dot(
            lead_cols, apply_incoming[0], preferred_element_type=jnp.float32
        ) + jnp.dot(trail_cols, apply_incoming[1], preferred_element_type=jnp.float32)
        product, picked_omega = (product, pick_rows(apply_incoming))
        reduced = (
            (stacked_samples.reshape(2 * local_rows, columns).astype(jnp.float32) - product)
            .astype(jnp.bfloat16)
            .reshape(2, local_rows, columns)
        )
        picked_samples = pick_rows(lax.all_gather(reduced, "grid", axis=1, tiled=True))
        rank_now = lax.dynamic_index_in_dim(ranks[height + 1], leaf_pos, 0, keepdims=False)
        current_samples = keep_alive(picked_samples.astype(jnp.bfloat16), rank_now, local_ids)
        current_omega = keep_alive(picked_omega.astype(jnp.bfloat16), rank_now, local_ids)
        coords = jnp.take(stacked_coords, pivots[height, 0], axis=1)
    return current_samples[None]


def solution(mesh):
    return jax.shard_map(
        body,
        mesh=mesh,
        in_specs=(
            P("leaf", "grid", None),
            P("leaf", "grid", None),
            P(None, "leaf", "grid"),
            P(),
            P(None, "leaf", None),
        ),
        out_specs=P("leaf", "grid", None),
        check_vma=False,
    )
```

profile of v0, /device:TPU:1, one launch (start us, length us, event | category | flops | bytes accessed | tf_op | source)
XLA Modules:
  0.0 209.2 jit_solution(15089806335397906216)
XLA Ops:
  6.5 0.8 fusion.61
  8.6 1.0 bitcast_select_fusion.1
  9.6 4.4 %collective-permute-start.2 = (bf16[32,1024]{1,0:T(8,128)(2,1)S(1)}, bf16[32,1024]{1,0:T(8,128)(2,1)S(1)}, u32[]{:S(2)}, u32[]{:S(2)}) collective-permute-start(bf16[32,1024]{1,0:T(8,128)(2,1)S(1)} %get-tuple-element.58), channel_id=1, source_target_pairs={{0,16},{16,0},{32,48},{48,32},{64,80},{80,64},{96,112},{112,96},{1... | collective-permute-start | bytes 196616 | tf_op jit(solution)/shard_map/ppermute | solution.py:11
  14.0 1.6 collective-permute-done.2
  15.6 0.7 pad_maximum_fusion.2
  16.3 0.8 copy.28
  17.1 23.5 %all_gather.15 = bf16[8,1,512]{0,1,2:T(2,128)(2,1)S(1)} all-gather(bf16[8,1,32]{0,1,2:T(2,128)(2,1)S(1)} %copy.28), channel_id=1, replica_groups=mesh['leaf'=32,'grid'=16] {'grid'}, dimensions={2}, use_global_device_ids=true | all-gather | bytes 8704 | tf_op jit(solution)/shard_map/all_gather | solution.py:44
  40.7 1.9 collective-permute-start.1
  42.6 3.4 %collective-permute-start = (bf16[32,1024]{1,0:T(8,128)(2,1)S(1)}, bf16[32,1024]{1,0:T(8,128)(2,1)S(1)}, u32[]{:S(2)}, u32[]{:S(2)}) collective-permute-start(bf16[32,1024]{1,0:T(8,128)(2,1)S(1)} %get-tuple-element.57), channel_id=1, source_target_pairs={{0,16},{16,0},{32,48},{48,32},{64,80},{80,64},{96,112},{112,96},{1... | collective-permute-start | bytes 196616 | tf_op jit(solution)/shard_map/ppermute | solution.py:11
  46.1 0.7 compare_select_fusion
  46.8 0.7 fusion.60
  47.8 1.3 gather_fusion
  49.2 3.5 %collective-permute-start.4 = (bf16[8,512]{0,1:T(8,128)(2,1)S(1)}, bf16[8,512]{0,1:T(8,128)(2,1)S(1)}, u32[]{:S(2)}, u32[]{:S(2)}) collective-permute-start(bf16[8,512]{0,1:T(8,128)(2,1)S(1)} %select_bitcast_fusion), channel_id=1, source_target_pairs={{0,32},{16,48},{32,0},{48,16},{64,96},{80,112},{96,64},{112,80},{1... | collective-permute-start | bytes 24584 | tf_op jit(solution)/shard_map/ppermute | solution.py:11
  53.4 6.5 %collective-permute-done.4 = bf16[8,512]{0,1:T(8,128)(2,1)S(1)} collective-permute-done((bf16[8,512]{0,1:T(8,128)(2,1)S(1)}, bf16[8,512]{0,1:T(8,128)(2,1)S(1)}, u32[]{:S(2)}, u32[]{:S(2)}) %collective-permute-start.4) | collective-permute-done | bytes 8224 | tf_op jit(solution)/shard_map/ppermute | solution.py:11
  61.4 2.5 %all-gather.5.cloned.1.call-done = bf16[2,512,1024]{2,1,0:T(8,128)(2,1)} async-done(((bf16[2,32,1024]{2,1,0:T(8,128)(2,1)}), bf16[2,512,1024]{2,1,0:T(8,128)(2,1)}) %all-gather.5.cloned.1.call-update) | async-done | bytes 2097168 | tf_op jit(solution)/shard_map/all_gather | solution.py:71
  63.9 1.7 fusion.15
  65.6 2.2 %fusion.2 = bf16[64,1024]{1,0:T(8,128)(2,1)} fusion(f32[64,1024]{1,0:T(8,128)S(1)} %fusion.15, bf16[2,512,1024]{2,1,0:T(8,128)(2,1)} %all-gather.5.cloned.1.call-done, bf16[64,1024]{1,0:T(8,128)(2,1)S(1)} %bitcast.87, bf16[64,1024]{1,0:T(8,128)(2,1)S(1)} %fusion.16), kind=kOutput, calls=%fused_computation.7 | convolution fusion | flops 67371008 | bytes 1638400 | tf_op jit(solution)/shard_map/dot_general | solution.py:77
  69.2 4.1 %collective-permute-start.5 = (bf16[32,1024]{1,0:T(8,128)(2,1)S(1)}, bf16[32,1024]{1,0:T(8,128)(2,1)S(1)}, u32[]{:S(2)}, u32[]{:S(2)}) collective-permute-start(bf16[32,1024]{1,0:T(8,128)(2,1)S(1)} %fusion.9), channel_id=1, source_target_pairs={{0,32},{16,48},{32,0},{48,16},{64,96},{80,112},{96,64},{112,80},{1... | collective-permute-start | bytes 196616 | tf_op jit(solution)/shard_map/ppermute | solution.py:11
  73.3 1.8 collective-permute-done.5
  75.2 0.7 pad_maximum_fusion.4
  76.1 1.2 convert_reduce_fusion.7
  77.3 32.3 %all-gather.7.cloned.1.call-done = bf16[2,512,1024]{2,1,0:T(8,128)(2,1)} async-done(((bf16[2,32,1024]{2,1,0:T(8,128)(2,1)}), bf16[2,512,1024]{2,1,0:T(8,128)(2,1)}) %all-gather.7.cloned.1.call-update) | async-done | bytes 2097168 | tf_op jit(solution)/shard_map/all_gather | solution.py:84
  109.6 1.5 fusion.13
  111.2 1.6 fusion.10
  112.7 4.2 %collective-permute-start.3 = (bf16[32,1024]{1,0:T(8,128)(2,1)S(1)}, bf16[32,1024]{1,0:T(8,128)(2,1)S(1)}, u32[]{:S(2)}, u32[]{:S(2)}) collective-permute-start(bf16[32,1024]{1,0:T(8,128)(2,1)S(1)} %fusion.10), channel_id=1, source_target_pairs={{0,32},{16,48},{32,0},{48,16},{64,96},{80,112},{96,64},{112,80},{1... | collective-permute-start | bytes 196616 | tf_op jit(solution)/shard_map/ppermute | solution.py:11
  117.3 1.4 collective-permute-done.3
  118.7 34.8 %all-gather.9.cloned.1.call-done = bf16[2,512,1024]{2,1,0:T(8,128)(2,1)} async-done(((bf16[2,32,1024]{2,1,0:T(8,128)(2,1)}), bf16[2,512,1024]{2,1,0:T(8,128)(2,1)}) %all-gather.9.cloned.1.call-update) | async-done | bytes 2097168 | tf_op jit(solution)/shard_map/all_gather | solution.py:71
  153.4 1.5 fusion.12
  155.0 2.2 %fusion.3 = bf16[64,1024]{1,0:T(8,128)(2,1)} fusion(f32[64,1024]{1,0:T(8,128)S(1)} %fusion.12, bf16[2,512,1024]{2,1,0:T(8,128)(2,1)} %all-gather.9.cloned.1.call-done, bf16[64,1024]{1,0:T(8,128)(2,1)S(1)} %bitcast.86, bf16[64,1024]{1,0:T(8,128)(2,1)S(1)} %fusion.17), kind=kOutput, calls=%fused_computation.8 | convolution fusion | flops 67371008 | bytes 1638400 | tf_op jit(solution)/shard_map/dot_general | solution.py:77
  158.5 40.5 %all-gather.11.cloned.1.call-done = bf16[2,512,1024]{2,1,0:T(8,128)(2,1)} async-done(((bf16[2,32,1024]{2,1,0:T(8,128)(2,1)}), bf16[2,512,1024]{2,1,0:T(8,128)(2,1)}) %all-gather.11.cloned.1.call-update) | async-done | bytes 2097168 | tf_op jit(solution)/shard_map/all_gather | solution.py:84
  199.0 1.5 fusion.11
  200.5 2.2 %fusion.8 = bf16[1,32,1024]{2,1,0:T(8,128)(2,1)} fusion(f32[32,1024]{1,0:T(8,128)S(1)} %fusion.11, bf16[2,512,1024]{2,1,0:T(8,128)(2,1)} %all-gather.11.cloned.1.call-done, pred[32]{0:T(512)(128)(4,1)S(1)} %broadcast_compare_fusion.2, s32[512]{0:T(512)S(1)} %iota_add_fusion, s32[32]{0:T(128)S(1)} %fusion.58), kind=kOutput, calls=%fused_computation.16 | convolution fusion | flops 33669120 | bytes 1247392 | tf_op jit(solution)/shard_map/dot_general | solution.py:67
  (49 shorter events, 7.4 us)
Async XLA Ops:
  6.5 57.4 %all-gather.5.cloned.1.call-start = ((), (), s32[]{:S(2)}) async-start(), calls=%async_computation | async-start | bytes 2228224 | tf_op jit(solution)/shard_map/all_gather | solution.py:71
  9.6 6.0 %collective-permute-start.2 = (bf16[32,1024]{1,0:T(8,128)(2,1)S(1)}, bf16[32,1024]{1,0:T(8,128)(2,1)S(1)}, u32[]{:S(2)}, u32[]{:S(2)}) collective-permute-start(bf16[32,1024]{1,0:T(8,128)(2,1)S(1)} %get-tuple-element.58), channel_id=1, source_target_pairs={{0,16},{16,0},{32,48},{48,32},{64,80},{80,64},{96,112},{112,96},{1... | collective-permute-start | bytes 196616 | tf_op jit(solution)/shard_map/ppermute | solution.py:11
  16.3 93.4 %all-gather.7.cloned.1.call-start = ((), (), s32[]{:S(2)}) async-start(), calls=%async_computation.1 | async-start | bytes 2228224 | tf_op jit(solution)/shard_map/all_gather | solution.py:84
  40.7 6.8 %collective-permute-start.1 = (bf16[8,512]{1,0:T(8,128)(2,1)S(1)}, bf16[8,512]{1,0:T(8,128)(2,1)S(1)}, u32[]{:S(2)}, u32[]{:S(2)}) collective-permute-start(bf16[8,512]{1,0:T(8,128)(2,1)S(1)} %bitcast.88), channel_id=1, source_target_pairs={{0,16},{16,0},{32,48},{48,32},{64,80},{80,64},{96,112},{112,96},{1... | collective-permute-start | bytes 24584 | tf_op jit(solution)/shard_map/ppermute | solution.py:11
  42.6 18.7 %collective-permute-start = (bf16[32,1024]{1,0:T(8,128)(2,1)S(1)}, bf16[32,1024]{1,0:T(8,128)(2,1)S(1)}, u32[]{:S(2)}, u32[]{:S(2)}) collective-permute-start(bf16[32,1024]{1,0:T(8,128)(2,1)S(1)} %get-tuple-element.57), channel_id=1, source_target_pairs={{0,16},{16,0},{32,48},{48,32},{64,80},{80,64},{96,112},{112,96},{1... | collective-permute-start | bytes 196616 | tf_op jit(solution)/shard_map/ppermute | solution.py:11
  49.2 10.6 %collective-permute-start.4 = (bf16[8,512]{0,1:T(8,128)(2,1)S(1)}, bf16[8,512]{0,1:T(8,128)(2,1)S(1)}, u32[]{:S(2)}, u32[]{:S(2)}) collective-permute-start(bf16[8,512]{0,1:T(8,128)(2,1)S(1)} %select_bitcast_fusion), channel_id=1, source_target_pairs={{0,32},{16,48},{32,0},{48,16},{64,96},{80,112},{96,64},{112,80},{1... | collective-permute-start | bytes 24584 | tf_op jit(solution)/shard_map/ppermute | solution.py:11
  63.9 4.6 %copy-start = (bf16[2,512,1024]{2,1,0:T(8,128)(2,1)S(1)}, bf16[2,512,1024]{2,1,0:T(8,128)(2,1)}, u32[]{:S(2)}) copy-start(bf16[2,512,1024]{2,1,0:T(8,128)(2,1)} %all-gather.5.cloned.1.call-done) | copy-start | bytes 6291460
  67.8 85.6 %all-gather.9.cloned.1.call-start = ((), (), s32[]{:S(2)}) async-start(), calls=%async_computation.2 | async-start | bytes 2228224 | tf_op jit(solution)/shard_map/all_gather | solution.py:71
  69.2 5.9 %collective-permute-start.5 = (bf16[32,1024]{1,0:T(8,128)(2,1)S(1)}, bf16[32,1024]{1,0:T(8,128)(2,1)S(1)}, u32[]{:S(2)}, u32[]{:S(2)}) collective-permute-start(bf16[32,1024]{1,0:T(8,128)(2,1)S(1)} %fusion.9), channel_id=1, source_target_pairs={{0,32},{16,48},{32,0},{48,16},{64,96},{80,112},{96,64},{112,80},{1... | collective-permute-start | bytes 196616 | tf_op jit(solution)/shard_map/ppermute | solution.py:11
  75.8 123.2 %all-gather.11.cloned.1.call-start = ((), (), s32[]{:S(2)}) async-start(), calls=%async_computation.3 | async-start | bytes 2228224 | tf_op jit(solution)/shard_map/all_gather | solution.py:84
  112.7 5.9 %collective-permute-start.3 = (bf16[32,1024]{1,0:T(8,128)(2,1)S(1)}, bf16[32,1024]{1,0:T(8,128)(2,1)S(1)}, u32[]{:S(2)}, u32[]{:S(2)}) collective-permute-start(bf16[32,1024]{1,0:T(8,128)(2,1)S(1)} %fusion.10), channel_id=1, source_target_pairs={{0,32},{16,48},{32,0},{48,16},{64,96},{80,112},{96,64},{112,80},{1... | collective-permute-start | bytes 196616 | tf_op jit(solution)/shard_map/ppermute | solution.py:11
Sparse Core Ops, SparseCore 0:
  16.4 47.4 all-gather.4
  67.9 41.6 all-gather.6
  111.8 41.6 all-gather.8
  157.3 41.6 all-gather.10
where the time goes:
time: 210 us; the launch traced here: 209 us
  waiting for transfers between devices  122 us (58%)
  blocking collectives  23.5 us (11%)
  starting transfers between devices  21.5 us (10%)
  matrix products  15 us (7%)
  between operations  13.4 us (6%)
  other arithmetic  7.84 us (4%)
  local copies, waits for them, and re-layouts  6.5 us (3%)
    all_gather x2, waiting for transfers between devices, body(): lax.all_gather(reduced, 'grid', axis=1, tiled=True)  72.8 us
    all_gather x2, waiting for transfers between devices, body(): apply_incoming = lax.all_gather(stacked_omega, 'grid', axis=1, tiled=True)  37.2 us
    all_gather x1, blocking collectives, body(): coords = lax.all_gather(points, 'grid', axis=2, tiled=True)[:, 0, :]  23.5 us
    ppermute x6, starting transfers between devices, from_partner(): lax.ppermute(x, axis, [(i, i ^ 1 << bit) for i in range(lax.axis_size(axi...  21.3 us
    ppermute x6, waiting for transfers between devices, from_partner(): lax.ppermute(x, axis, [(i, i ^ 1 << bit) for i in range(lax.axis_size(axi...  11.4 us
    dot_general x2, matrix products, body(): jnp.dot(trail_cols, apply_incoming[1], preferred_element_type=jnp.float32)  4.35 us
  transfers between devices with their start and end apart: 10, of which 8 were waited for; matrix products, arithmetic and copies ran while one was open for 7% of the time, Pallas kernels for 0%

commit v1 on v0

v1 whole, which is shorter than its diff:
```python
import functools
import math

import jax
import jax.numpy as jnp
from jax import lax
from jax.experimental import pallas as pl
from jax.experimental.pallas import tpu as pltpu
from jax.sharding import PartitionSpec as P

MESH = pl.DeviceIdType.MESH
BF = jnp.bfloat16
F32 = jnp.float32
I32 = jnp.int32
kernel_rate = 0.6

WORKERS = [(0, 0, 0), (1, 0, 0), (0, 0, 1), (1, 0, 1), (0, 0, 2), (1, 0, 2), (0, 0, 3), (1, 0, 3)]
SEND_ORDER = list(range(8))
FAR_FIRST = sorted(range(32), key=lambda c: -(c // 8 * 10 + min(c // 2 % 4, 4 - c // 2 % 4) * 2 + c % 2))


def total(flags):
    return functools.reduce(lambda a, b: a + b, flags)


def kernel(
    samples, omega, points, ranks, pivots, out,
    pts_v, piv_v, rank_s, meta_out, meta_in, om_in, sa_in, pick, mat, lift, lift_in, part, part_in, blocks,
    local_sem, send_sem, recv_sem, pair_sem,
):
    leaf = lax.axis_index("leaf")
    grid = lax.axis_index("grid")
    core = grid % 2
    x = grid // 4
    y = (grid // 2) % 2
    z = leaf % 4
    base = leaf - z
    y_flip = (leaf // 16) % 2
    z_flip = 3 * ((leaf % 16) // 8)
    ny = (y + y_flip) % 2
    nz = z + (z_flip // 3) * (3 - 2 * z)
    chip = nz * 8 + x * 2 + ny

    def device(number):
        cx, cy, cz = number // 2 % 4, number % 2, number // 8
        at_z = cz + (z_flip // 3) * (3 - 2 * cz)
        at_y = (cy + y_flip) % 2
        return (base + at_z, cx * 4 + at_y * 2 + core)

    worker_chips = [wz * 8 + wx * 2 + wy for wx, wy, wz in WORKERS]
    mine = total([jnp.where(chip == c, i + 1, 0) for i, c in enumerate(worker_chips)])
    is_worker = mine > 0
    slot = jnp.maximum(mine - 1, 0)
    my_columns = pl.ds(pl.multiple_of(slot * 128, 128), 128)
    peer = (leaf, grid + 1 - 2 * core)

    loads = [
        pltpu.make_async_copy(points, pts_v, local_sem.at[0]),
        pltpu.make_async_copy(pivots, piv_v, local_sem.at[1]),
        pltpu.make_async_copy(ranks, rank_s, local_sem.at[2]),
    ]
    for load in loads:
        load.start()

    barrier = pltpu.get_barrier_semaphore()

    @pl.when(is_worker)
    def _():
        for number in FAR_FIRST:

            @pl.when(chip != number)
            def _():
                pl.semaphore_signal(barrier, inc=1, device_id=device(number), device_id_type=MESH)

        pl.semaphore_signal(barrier, inc=1, device_id=peer, device_id_type=MESH)
        own = [
            pltpu.make_async_copy(omega.at[0, :, my_columns], om_in.at[chip], recv_sem.at[1]),
            pltpu.make_async_copy(samples.at[0, :, my_columns], sa_in.at[chip], recv_sem.at[2]),
        ]
        for copy in own:
            copy.start()

    for load in loads:
        load.wait()

    first_rank = rank_s[0, leaf]
    kept_rank = rank_s[1, leaf]
    child = (z // 2) % 2
    first_pivots = piv_v[0]
    last_pivots = piv_v[1]
    row = lax.broadcasted_iota(I32, (32, 512), 0)
    lane = lax.broadcasted_iota(I32, (32, 512), 1)
    own_row = (z % 2) * 512 + grid * 32 + row
    place = jnp.sum(jnp.where(first_pivots == own_row, lane + 1, 0).astype(F32), axis=1, keepdims=True)
    target = jnp.where(place > 0.5, child.astype(F32) * 512.0 + place - 1.0, -1.0)
    final = (
        jnp.sum(jnp.where(last_pivots.astype(F32) == target, lane + 1, 0).astype(F32), axis=1, keepdims=True) - 1.0
    )
    column = lax.broadcasted_iota(I32, (32, 1), 0)
    alive = (grid * 32 + column < first_rank).astype(F32)
    kept = alive * ((place > 0.5) & (place < kept_rank.astype(F32) + 0.5)).astype(F32)
    side = child.astype(F32)
    high = jnp.floor((final + 1.0) * (1.0 / 32.0))
    low = final + 1.0 - 32.0 * high
    field = lax.broadcasted_iota(I32, (32, 128), 1)
    fields = jnp.where(field == 11, side, 0.0)
    fields = jnp.where(field == 12, alive * (1.0 - side) + kept, fields)
    fields = jnp.where(field == 13, alive * (2.0 * side - 1.0), fields)
    fields = jnp.where(field == 14, high, fields)
    fields = jnp.where(field == 15, low, fields)
    coords = pts_v[:, 0, :].astype(F32)
    norm = jnp.sum(coords * coords, axis=0, keepdims=True)
    norm_a = norm.astype(BF).astype(F32)
    norm_b = (norm - norm_a).astype(BF).astype(F32)
    norm_c = norm - norm_a - norm_b
    sub = lax.broadcasted_iota(I32, (8, 32), 0)
    norms = jnp.where(sub == 0, norm_a, jnp.where(sub == 1, norm_b, jnp.where(sub == 2, norm_c, 0.0)))
    upper = jnp.concatenate([coords, norms], axis=0).astype(BF)
    spot = (
        lax.broadcasted_iota(I32, (32, 128), 1) == lax.broadcasted_iota(I32, (32, 128), 0) + (chip % 4) * 32
    ).astype(BF)
    tile = jnp.dot(upper, spot, preferred_element_type=F32)
    lower = lax.dot_general(fields.astype(BF), spot, (((0,), (0,)), ((), ())), preferred_element_type=F32)
    meta_out[...] = (tile + lower[0:16]).astype(BF)

    @pl.when(is_worker)
    def _():
        copy = pltpu.make_async_copy(meta_out, meta_in.at[chip], recv_sem.at[0])
        copy.start()

    pl.semaphore_wait(barrier, 8)

    def send_all(source, target_ref, number):
        for w in SEND_ORDER:

            @pl.when(chip != worker_chips[w])
            def _():
                pltpu.make_async_remote_copy(
                    src_ref=source(w),
                    dst_ref=target_ref.at[chip],
                    send_sem=send_sem.at[number],
                    recv_sem=recv_sem.at[number],
                    device_id=device(worker_chips[w]),
                    device_id_type=MESH,
                ).start()

    send_all(lambda w: meta_out, meta_in, 0)
    send_all(lambda w: omega.at[0, :, pl.ds(128 * w, 128)], om_in, 1)
    send_all(lambda w: samples.at[0, :, pl.ds(128 * w, 128)], sa_in, 2)

    def await_bytes(ref, sem):
        pltpu.make_async_copy(ref, ref, sem).wait()

    @pl.when(is_worker)
    def _():
        await_bytes(meta_in, recv_sem.at[0])
        tiles = []
        for group in range(8):
            tiles.append(total([meta_in[4 * group + q].astype(F32) for q in range(4)]))
        meta = jnp.concatenate(tiles, axis=1)
        position = meta[14:15] * 32.0 + meta[15:16] - 1.0
        part_row = lax.broadcasted_iota(I32, (16, 1024), 0)
        right = jnp.where(part_row < 11, meta, jnp.where(part_row < 14, 1.0, 0.0)).astype(BF)
        shift = jnp.concatenate([meta[13:16], meta[0:13]], axis=0)
        raised = jnp.where(
            part_row < 8, -2.0 * meta, jnp.where((part_row >= 11) & (part_row < 14), shift, 0.0)
        )
        raised = jnp.where(part_row == 14, meta[11:12], raised).astype(BF)
        factor = jnp.where(part_row == 14, meta[13:14], jnp.where(part_row == 15, meta[12:13], 0.0)).astype(BF)

        for chunk in range(8):
            line = lax.broadcasted_iota(I32, (64, 1), 0) + 64 * chunk
            order = (line % 256) // 32 * 64 + line // 256 * 32 + line % 32
            hit = (position == order.astype(F32)).astype(BF)
            pick[pl.ds(64 * chunk, 64), :] = hit
        picked = lax.dot_general(pick[...], raised, (((1,), (1,)), ((), ())), preferred_element_type=F32)
        lift[:, 0:16] = picked.astype(BF)
        swap = pltpu.make_async_remote_copy(
            src_ref=lift, dst_ref=lift_in, send_sem=pair_sem.at[0], recv_sem=pair_sem.at[1],
            device_id=peer, device_id_type=MESH,
        )
        swap.start()
        swap.wait_recv()
        spread = lax.broadcasted_iota(I32, (512, 16), 1)
        ones = ((spread >= 8) & (spread < 11)) | (spread == 15)
        left = picked + lift_in[:, 0:16].astype(F32) + jnp.where(ones, 1.0, 0.0)
        left = left.astype(BF)
        scale = -kernel_rate * math.log2(math.e)
        for chunk in range(8):
            rows = slice(64 * chunk, 64 * chunk + 64)
            distance = jnp.dot(left[rows], right, preferred_element_type=F32)
            coef = jnp.dot(left[rows], factor, preferred_element_type=F32)
            diagonal = pick[rows, :].astype(F32)
            entry = (jnp.exp2(distance * scale) + diagonal).astype(BF)
            mat[rows, :] = entry * coef.astype(BF)

        await_bytes(om_in, recv_sem.at[1])
        product = jnp.dot(mat[...], om_in[...].reshape(1024, 128), preferred_element_type=F32)
        await_bytes(sa_in, recv_sem.at[2])
        chosen = jnp.dot(pick[...], sa_in[...].reshape(1024, 128), preferred_element_type=F32)
        part[...] = chosen - product
        trade = pltpu.make_async_remote_copy(
            src_ref=part.at[pl.ds(pl.multiple_of(256 * (1 - core), 256), 256)], dst_ref=part_in,
            send_sem=pair_sem.at[2], recv_sem=pair_sem.at[3], device_id=peer, device_id_type=MESH,
        )
        trade.start()
        trade.wait_recv()
        last_rank = rank_s[2, leaf]
        mine_rows = part[pl.ds(pl.multiple_of(256 * core, 256), 256)] + part_in[...]
        line = lax.broadcasted_iota(I32, (256, 128), 0)
        order = line // 32 * 64 + core * 32 + line % 32
        mine_rows = jnp.where(order < last_rank, mine_rows, 0.0).astype(BF)
        blocks[...] = mine_rows.reshape(8, 32, 128)

        for number in FAR_FIRST[::-1]:
            block = blocks.at[number // 2 % 4 * 2 + (number % 2 + y_flip) % 2]

            @pl.when(chip != number)
            def _():
                pltpu.make_async_remote_copy(
                    src_ref=block,
                    dst_ref=out.at[0, :, my_columns],
                    send_sem=send_sem.at[3],
                    recv_sem=recv_sem.at[3],
                    device_id=device(number),
                    device_id_type=MESH,
                ).start()

        pltpu.make_async_copy(blocks.at[x * 2 + y], out.at[0, :, my_columns], recv_sem.at[3]).start()

    await_bytes(out, recv_sem.at[3])

    @pl.when(is_worker)
    def _():
        swap = pltpu.make_async_copy(lift, lift_in, pair_sem.at[0])
        swap.wait()
        trade = pltpu.make_async_copy(part_in, part_in, pair_sem.at[2])
        trade.wait()
        await_bytes(om_in.at[pl.ds(0, 31)], send_sem.at[3])
        await_bytes(meta_in.at[pl.ds(0, 7)], send_sem.at[0])
        await_bytes(om_in.at[pl.ds(0, 7)], send_sem.at[1])
        await_bytes(sa_in.at[pl.ds(0, 7)], send_sem.at[2])

    @pl.when(jnp.logical_not(is_worker))
    def _():
        await_bytes(meta_in.at[pl.ds(0, 8)], send_sem.at[0])
        await_bytes(om_in.at[pl.ds(0, 8)], send_sem.at[1])
        await_bytes(sa_in.at[pl.ds(0, 8)], send_sem.at[2])


def body(samples, omega, points, ranks, pivots):
    anywhere = pl.BlockSpec(memory_space=pl.ANY)
    return pl.pallas_call(
        kernel,
        out_shape=jax.ShapeDtypeStruct((1, 32, 1024), BF),
        in_specs=[anywhere] * 5,
        out_specs=pl.BlockSpec(memory_space=pltpu.VMEM),
        scratch_shapes=[
            pltpu.VMEM((8, 1, 32), BF),
            pltpu.VMEM((2, 1, 512), I32),
            pltpu.SMEM((3, 32), I32),
            pltpu.VMEM((16, 128), BF),
            pltpu.VMEM((32, 16, 128), BF),
            pltpu.VMEM((32, 32, 128), BF),
            pltpu.VMEM((32, 32, 128), BF),
            pltpu.VMEM((512, 1024), BF),
            pltpu.VMEM((512, 1024), BF),
            pltpu.VMEM((512, 128), BF),
            pltpu.VMEM((512, 128), BF),
            pltpu.VMEM((512, 128), F32),
            pltpu.VMEM((256, 128), F32),
            pltpu.VMEM((8, 32, 128), BF),
            pltpu.SemaphoreType.DMA((3,)),
            pltpu.SemaphoreType.DMA((4,)),
            pltpu.SemaphoreType.DMA((4,)),
            pltpu.SemaphoreType.DMA((4,)),
        ],
        compiler_params=pltpu.CompilerParams(
            collective_id=0, has_side_effects=True, vmem_limit_bytes=40 * 2**20
        ),
        cost_estimate=pl.CostEstimate(flops=300_000_000, bytes_accessed=200_000, transcendentals=524288),
    )(samples, omega, points, ranks, pivots)


def solution(mesh):
    return jax.shard_map(
        body,
        mesh=mesh,
        in_specs=(
            P("leaf", "grid", None),
            P("leaf", "grid", None),
            P(None, "leaf", "grid"),
            P(),
            P(None, "leaf", None),
        ),
        out_specs=P("leaf", "grid", None),
        check_vma=False,
    )
```

time: 210 us -> 29.7 us (0.14)
  the two profiles are of different devices: /device:TPU:1 before, /device:TPU:20 now
where the time goes in v1:
time: 29.7 us; the launch traced here: 29.5 us
  Pallas kernels  26.4 us (89%)
  local copies, waits for them, and re-layouts  3.03 us (10%)
    pallas_call x1, Pallas kernels, body(): pl.pallas_call(kernel, out_shape=jax.ShapeDtypeStruct((1, 32, 1024), BF),...  26.4 us
    unnamed x10, local copies, waits for them, and re-layouts  3.03 us

profile of v1, /device:TPU:20, one launch (start us, length us, event | category | flops | bytes accessed | tf_op | source)
XLA Modules:
  0.0 29.5 jit_solution(17975716700063113123)
XLA Ops:
  0.0 0.0 copy-start.2
  0.0 0.0 copy-start.3
  0.0 0.7 %copy.6.points = bf16[8,1,32]{2,1,0:T(2,128)(2,1)S(1)} copy(bf16[8,1,32]{2,0,1:T(8,128)(2,1)} %param.7) | data formatting | bytes 1024 | tf_op args[2]
  0.7 0.0 copy-done.2
  0.7 0.0 copy-done.3
  0.7 0.0 copy-start
  0.7 0.8 %copy-done = bf16[1,32,1024]{2,1,0:T(8,128)(2,1)S(1)} copy-done((bf16[1,32,1024]{2,1,0:T(8,128)(2,1)S(1)}, bf16[1,32,1024]{2,1,0:T(8,128)(2,1)}, u32[]{:S(2)}) %copy-start) | copy-done | bytes 65560
  1.6 0.0 copy-start.1
  1.6 0.8 %copy-done.1 = bf16[1,32,1024]{2,1,0:T(8,128)(2,1)S(1)} copy-done((bf16[1,32,1024]{2,1,0:T(8,128)(2,1)S(1)}, bf16[1,32,1024]{2,1,0:T(8,128)(2,1)}, u32[]{:S(2)}) %copy-start.1) | copy-done | bytes 65560
  2.4 26.4 %shard_map.55 = bf16[1,32,1024]{2,1,0:T(8,128)(2,1)S(1)} custom-call(bf16[1,32,1024]{2,1,0:T(8,128)(2,1)S(1)} %copy-done, bf16[1,32,1024]{2,1,0:T(8,128)(2,1)S(1)} %copy-done.1, bf16[8,1,32]{2,1,0:T(2,128)(2,1)S(1)} %copy.6.points, s32[3,32]{1,0:T(4,128)S(1)} %copy-done.3, s32[2,1,512]{2,1,0:T(1,128)S(1)} %copy-done.2), custom_call_target="tpu_custom_call" | custom-call | flops 300000000 | bytes 200000 | tf_op jit(solution)/shard_map/pallas_call | solution.py:253
  28.9 0.6 %copy.8 = bf16[1,32,1024]{2,1,0:T(8,128)(2,1)} copy(bf16[1,32,1024]{2,1,0:T(8,128)(2,1)S(1)} %shard_map.55) | data formatting | bytes 131072
Async XLA Ops:
  0.0 0.7 %copy-start.2 = (s32[2,1,512]{2,1,0:T(1,128)S(1)}, s32[2,1,512]{2,1,0:T(1,128)}, u32[]{:S(2)}) copy-start(s32[2,1,512]{2,1,0:T(1,128)} %pivots.1) | copy-start | bytes 12292
  0.0 0.7 %copy-start.3 = (s32[3,32]{1,0:T(4,128)S(1)}, s32[3,32]{1,0:T(4,128)}, u32[]{:S(2)}) copy-start(s32[3,32]{1,0:T(4,128)} %ranks.1) | copy-start | bytes 1156
  0.7 0.8 %copy-start = (bf16[1,32,1024]{2,1,0:T(8,128)(2,1)S(1)}, bf16[1,32,1024]{2,1,0:T(8,128)(2,1)}, u32[]{:S(2)}) copy-start(bf16[1,32,1024]{2,1,0:T(8,128)(2,1)} %samples.1) | copy-start | bytes 196612
  1.6 0.8 %copy-start.1 = (bf16[1,32,1024]{2,1,0:T(8,128)(2,1)S(1)}, bf16[1,32,1024]{2,1,0:T(8,128)(2,1)}, u32[]{:S(2)}) copy-start(bf16[1,32,1024]{2,1,0:T(8,128)(2,1)} %omega.1) | copy-start | bytes 196612

commit v2 on v1

--- a/solution.py
+++ b/solution.py
@@ -14,7 +14,7 @@
 I32 = jnp.int32
 kernel_rate = 0.6
 
-WORKERS = [(0, 0, 0), (1, 0, 0), (0, 0, 1), (1, 0, 1), (0, 0, 2), (1, 0, 2), (0, 0, 3), (1, 0, 3)]
+WORKERS = [(0,0,0),(1,0,1),(2,0,0),(3,0,1),(0,0,2),(1,1,0),(0,1,1),(3,1,0)]
 SEND_ORDER = list(range(8))
 FAR_FIRST = sorted(range(32), key=lambda c: -(c // 8 * 10 + min(c // 2 % 4, 4 - c // 2 % 4) * 2 + c % 2))
 
@@ -108,7 +108,7 @@
     fields = jnp.where(field == 13, alive * (2.0 * side - 1.0), fields)
     fields = jnp.where(field == 14, high, fields)
     fields = jnp.where(field == 15, low, fields)
-    coords = pts_v[:, 0, :].astype(F32)
+    coords = pts_v[...].astype(F32)
     norm = jnp.sum(coords * coords, axis=0, keepdims=True)
     norm_a = norm.astype(BF).astype(F32)
     norm_b = (norm - norm_a).astype(BF).astype(F32)
@@ -145,8 +145,8 @@
                 ).start()
 
     send_all(lambda w: meta_out, meta_in, 0)
+    send_all(lambda w: samples.at[0, :, pl.ds(128 * w, 128)], sa_in, 2)
     send_all(lambda w: omega.at[0, :, pl.ds(128 * w, 128)], om_in, 1)
-    send_all(lambda w: samples.at[0, :, pl.ds(128 * w, 128)], sa_in, 2)
 
     def await_bytes(ref, sem):
         pltpu.make_async_copy(ref, ref, sem).wait()
@@ -169,24 +169,29 @@
         factor = jnp.where(part_row == 14, meta[13:14], jnp.where(part_row == 15, meta[12:13], 0.0)).astype(BF)
 
         for chunk in range(8):
-            line = lax.broadcasted_iota(I32, (64, 1), 0) + 64 * chunk
-            order = (line % 256) // 32 * 64 + line // 256 * 32 + line % 32
+            line = lax.broadcasted_iota(I32, (64, 1), 0) + 64 * (chunk % 4)
+            half = 1 - core if chunk < 4 else core
+            order = line // 32 * 64 + half * 32 + line % 32
             hit = (position == order.astype(F32)).astype(BF)
             pick[pl.ds(64 * chunk, 64), :] = hit
         picked = lax.dot_general(pick[...], raised, (((1,), (1,)), ((), ())), preferred_element_type=F32)
-        lift[:, 0:16] = picked.astype(BF)
+        lift[0:256, 0:16] = picked[256:512].astype(BF)
+        lift[256:512, 0:16] = picked[0:256].astype(BF)
         swap = pltpu.make_async_remote_copy(
             src_ref=lift, dst_ref=lift_in, send_sem=pair_sem.at[0], recv_sem=pair_sem.at[1],
             device_id=peer, device_id_type=MESH,
         )
         swap.start()
+        await_bytes(sa_in, recv_sem.at[2])
+        part[...] = jnp.dot(pick[...], sa_in[...].reshape(1024, 128), preferred_element_type=F32)
         swap.wait_recv()
         spread = lax.broadcasted_iota(I32, (512, 16), 1)
         ones = ((spread >= 8) & (spread < 11)) | (spread == 15)
         left = picked + lift_in[:, 0:16].astype(F32) + jnp.where(ones, 1.0, 0.0)
         left = left.astype(BF)
         scale = -kernel_rate * math.log2(math.e)
-        for chunk in range(8):
+
+        def form(chunk):
             rows = slice(64 * chunk, 64 * chunk + 64)
             distance = jnp.dot(left[rows], right, preferred_element_type=F32)
             coef = jnp.dot(left[rows], factor, preferred_element_type=F32)
@@ -194,19 +199,21 @@
             entry = (jnp.exp2(distance * scale) + diagonal).astype(BF)
             mat[rows, :] = entry * coef.astype(BF)
 
+        for chunk in range(4):
+            form(chunk)
         await_bytes(om_in, recv_sem.at[1])
-        product = jnp.dot(mat[...], om_in[...].reshape(1024, 128), preferred_element_type=F32)
-        await_bytes(sa_in, recv_sem.at[2])
-        chosen = jnp.dot(pick[...], sa_in[...].reshape(1024, 128), preferred_element_type=F32)
-        part[...] = chosen - product
+        part[0:256] -= jnp.dot(mat[0:256], om_in[...].reshape(1024, 128), preferred_element_type=F32)
         trade = pltpu.make_async_remote_copy(
-            src_ref=part.at[pl.ds(pl.multiple_of(256 * (1 - core), 256), 256)], dst_ref=part_in,
+            src_ref=part.at[pl.ds(0, 256)], dst_ref=part_in,
             send_sem=pair_sem.at[2], recv_sem=pair_sem.at[3], device_id=peer, device_id_type=MESH,
         )
         trade.start()
+        for chunk in range(4, 8):
+            form(chunk)
+        part[256:512] -= jnp.dot(mat[256:512], om_in[...].reshape(1024, 128), preferred_element_type=F32)
         trade.wait_recv()
         last_rank = rank_s[2, leaf]
-        mine_rows = part[pl.ds(pl.multiple_of(256 * core, 256), 256)] + part_in[...]
+        mine_rows = part[256:512] + part_in[...]
         line = lax.broadcasted_iota(I32, (256, 128), 0)
         order = line // 32 * 64 + core * 32 + line % 32
         mine_rows = jnp.where(order < last_rank, mine_rows, 0.0).astype(BF)
@@ -252,11 +259,11 @@
     anywhere = pl.BlockSpec(memory_space=pl.ANY)
     return pl.pallas_call(
         kernel,
-        out_shape=jax.ShapeDtypeStruct((1, 32, 1024), BF),
+        out_shape=pltpu.VMEM((1, 32, 1024), BF),
         in_specs=[anywhere] * 5,
         out_specs=pl.BlockSpec(memory_space=pltpu.VMEM),
         scratch_shapes=[
-            pltpu.VMEM((8, 1, 32), BF),
+            pltpu.VMEM((8, 32), BF),
             pltpu.VMEM((2, 1, 512), I32),
             pltpu.SMEM((3, 32), I32),
             pltpu.VMEM((16, 128), BF),
@@ -276,10 +283,10 @@
             pltpu.SemaphoreType.DMA((4,)),
         ],
         compiler_params=pltpu.CompilerParams(
-            collective_id=0, has_side_effects=True, vmem_limit_bytes=40 * 2**20
+            collective_id=0, has_side_effects=True, vmem_limit_bytes=60 * 2**20
         ),
         cost_estimate=pl.CostEstimate(flops=300_000_000, bytes_accessed=200_000, transcendentals=524288),
-    )(samples, omega, points, ranks, pivots)
+    )(samples, omega, points[:, 0, :], ranks, pivots)
 
 
 def solution(mesh):

time: 29.7 us -> 26.6 us (0.90)
  the two profiles are of different devices: /device:TPU:20 before, /device:TPU:256 now
where the time goes in v2:
time: 26.6 us; the launch traced here: 26.4 us
  Pallas kernels  25.8 us (97%)
  local copies, waits for them, and re-layouts  0.63 us (2%)
    pallas_call x1, Pallas kernels, body(): pl.pallas_call(kernel, out_shape=pltpu.VMEM((1, 32, 1024), BF), in_specs=...  25.8 us
    unnamed x1, local copies, waits for them, and re-layouts  0.63 us

profile of v2, /device:TPU:256, one launch (start us, length us, event | category | flops | bytes accessed | tf_op | source)
XLA Modules:
  0.0 26.4 jit_solution(4471457798116343357)
XLA Ops:
  0.0 25.8 %shard_map.55 = bf16[1,32,1024]{2,1,0:T(8,128)(2,1)S(1)} custom-call(bf16[1,32,1024]{2,1,0:T(8,128)(2,1)} %samples.1, bf16[1,32,1024]{2,1,0:T(8,128)(2,1)} %omega.1, bf16[8,32]{1,0:T(8,128)(2,1)} %bitcast.1, s32[3,32]{1,0:T(4,128)} %ranks.1, s32[2,1,512]{2,1,0:T(1,128)} %pivots.1), custom_call_target="tpu_custom_call" | custom-call | flops 300000000 | bytes 200000 | tf_op jit(solution)/shard_map/pallas_call | solution.py:260
  25.8 0.6 %copy.7 = bf16[1,32,1024]{2,1,0:T(8,128)(2,1)} copy(bf16[1,32,1024]{2,1,0:T(8,128)(2,1)S(1)} %shard_map.55) | data formatting | bytes 131072

commit v3 on v2

v3 whole, which is shorter than its diff:
```python
import functools
import math

import jax
import jax.numpy as jnp
from jax import lax
from jax.experimental import pallas as pl
from jax.experimental.pallas import tpu as pltpu
from jax.sharding import PartitionSpec as P

MESH = pl.DeviceIdType.MESH
BF = jnp.bfloat16
F32 = jnp.float32
I32 = jnp.int32
kernel_rate = 0.6

NEAR = [z * 8 + x * 2 + y for y, z in [(0, 0), (0, 1), (0, 2), (1, 0)] for x in (0, 1, 3, 2)]
MIDDLE = [p * 8 + c for p in (0, 1) for c in range(8)]
PLANES = [1, 2, 0, 3]
FAR_FIRST = sorted(range(32), key=lambda c: -(c // 8 * 10 + min(c // 2 % 4, 4 - c // 2 % 4) * 2 + c % 2))
OUT_ORDER = [p * 8 + c for c in [0, 2, 6, 1, 4, 3, 7, 5] for p in [0, 3, 2, 1]]


def total(flags):
    return functools.reduce(lambda a, b: a + b, flags)


def kernel(
    samples, omega, points, ranks, pivots, out,
    pts_v, piv_v, rank_s, om_v, sa_v, packed, meta_out, meta_in, meta_turn, data_in, pick, mat, lift, lift_in, part, part_in,
    blocks, pieces,
    local_sem, send_sem, recv_sem, pair_sem,
):
    leaf = lax.axis_index("leaf")
    grid = lax.axis_index("grid")
    core = grid % 2
    x = grid // 4
    y = (grid // 2) % 2
    z = leaf % 4
    base = leaf - z
    back = (leaf % 16) // 8
    plane = total([jnp.where(z == k + back * (PLANES[k] - k), k, 0) for k in range(4)])
    chip = plane * 8 + x * 2 + y

    def device(number):
        cx, cy, cz = number // 2 % 4, number % 2, number // 8
        return (base + cz + back * (PLANES[cz] - cz), cx * 4 + cy * 2 + core)

    def worker(w):
        a, b = NEAR[w], MIDDLE[w]
        plane_a, plane_b = a // 8, PLANES[b // 8]
        return (base + plane_a + back * (plane_b - plane_a), (a % 8 + back * (b % 8 - a % 8)) * 2 + core)

    worker_chips = [a + back * (b - a) for a, b in zip(NEAR, MIDDLE, strict=True)]
    mine = total([jnp.where(chip == c, i + 1, 0) for i, c in enumerate(worker_chips)])
    is_worker = mine > 0
    slot = jnp.maximum(mine - 1, 0)
    meta_slot = chip % 4 * 8 + chip // 4
    peer = (leaf, grid + 1 - 2 * core)

    loads = [
        pltpu.make_async_copy(omega.at[0], om_v, local_sem.at[3]),
        pltpu.make_async_copy(samples.at[0], sa_v, local_sem.at[4]),
        pltpu.make_async_copy(points, pts_v, local_sem.at[0]),
        pltpu.make_async_copy(pivots, piv_v, local_sem.at[1]),
        pltpu.make_async_copy(ranks, rank_s, local_sem.at[2]),
    ]
    for load in loads:
        load.start()

    barrier = pltpu.get_barrier_semaphore()

    @pl.when(is_worker)
    def _():
        for number in FAR_FIRST:

            @pl.when(chip != number)
            def _():
                pl.semaphore_signal(barrier, inc=1, device_id=device(number), device_id_type=MESH)

        pl.semaphore_signal(barrier, inc=1, device_id=peer, device_id_type=MESH)

    for load in loads:
        load.wait()

    first_rank = rank_s[0, leaf]
    kept_rank = rank_s[1, leaf]
    child = (z // 2) % 2
    first_pivots = piv_v[0]
    last_pivots = piv_v[1]
    row = lax.broadcasted_iota(I32, (32, 512), 0)
    lane = lax.broadcasted_iota(I32, (32, 512), 1)
    own_row = (z % 2) * 512 + grid * 32 + row
    place = jnp.sum(jnp.where(first_pivots == own_row, lane + 1, 0).astype(F32), axis=1, keepdims=True)
    target = jnp.where(place > 0.5, child.astype(F32) * 512.0 + place - 1.0, -1.0)
    final = (
        jnp.sum(jnp.where(last_pivots.astype(F32) == target, lane + 1, 0).astype(F32), axis=1, keepdims=True) - 1.0
    )
    column = lax.broadcasted_iota(I32, (32, 1), 0)
    alive = (grid * 32 + column < first_rank).astype(F32)
    kept = alive * ((place > 0.5) & (place < kept_rank.astype(F32) + 0.5)).astype(F32)
    side = child.astype(F32)
    high = jnp.floor((final + 1.0) * (1.0 / 32.0))
    low = final + 1.0 - 32.0 * high
    field = lax.broadcasted_iota(I32, (32, 128), 1)
    fields = jnp.where(field == 11, side, 0.0)
    fields = jnp.where(field == 12, alive * (1.0 - side) + kept, fields)
    fields = jnp.where(field == 13, alive * (2.0 * side - 1.0), fields)
    fields = jnp.where(field == 14, high, fields)
    fields = jnp.where(field == 15, low, fields)
    coords = pts_v[...].astype(F32)
    norm = jnp.sum(coords * coords, axis=0, keepdims=True)
    norm_a = norm.astype(BF).astype(F32)
    norm_b = (norm - norm_a).astype(BF).astype(F32)
    norm_c = norm - norm_a - norm_b
    sub = lax.broadcasted_iota(I32, (8, 32), 0)
    norms = jnp.where(sub == 0, norm_a, jnp.where(sub == 1, norm_b, jnp.where(sub == 2, norm_c, 0.0)))
    upper = jnp.concatenate([coords, norms], axis=0).astype(BF)
    repeat = (
        lax.broadcasted_iota(I32, (32, 128), 1) % 32 == lax.broadcasted_iota(I32, (32, 128), 0)
    ).astype(BF)
    tile = jnp.dot(upper, repeat, preferred_element_type=F32)
    lower = lax.dot_general(fields.astype(BF), repeat, (((0,), (0,)), ((), ())), preferred_element_type=F32)
    tile = tile + lower[0:16]
    at_field = lax.broadcasted_iota(I32, (16, 128), 0)
    at_block = lax.broadcasted_iota(I32, (16, 128), 1) // 32
    for part_of in range(4):
        chosen_row = jnp.where(at_field == 4 * part_of + at_block, tile, 0.0)
        meta_out[:, 128 * part_of : 128 * part_of + 128] = jnp.sum(chosen_row, axis=0, keepdims=True)

    left_half = lax.broadcasted_iota(I32, (32, 128), 1) < 64
    for v in range(8):
        o = om_v[:, 128 * v : 128 * v + 128].astype(F32)
        a = sa_v[:, 128 * v : 128 * v + 128].astype(F32)
        packed[2 * v] = jnp.where(left_half, o, pltpu.roll(a, 64, 1)).astype(BF)
        packed[2 * v + 1] = jnp.where(left_half, pltpu.roll(o, 64, 1), a).astype(BF)

    @pl.when(is_worker)
    def _():
        pltpu.make_async_copy(meta_out, meta_in.at[meta_slot], recv_sem.at[0]).start()
        pltpu.make_async_copy(packed.at[slot], data_in.at[chip], recv_sem.at[1]).start()

    pl.semaphore_wait(barrier, 16)

    def send_all(source, target, number):
        for w in range(16):

            @pl.when(chip != worker_chips[w])
            def _():
                pltpu.make_async_remote_copy(
                    src_ref=source(w),
                    dst_ref=target,
                    send_sem=send_sem.at[number],
                    recv_sem=recv_sem.at[number],
                    device_id=worker(w),
                    device_id_type=MESH,
                ).start()

    send_all(lambda w: meta_out, meta_in.at[meta_slot], 0)
    send_all(lambda w: packed.at[w], data_in.at[chip], 1)

    def await_bytes(ref, sem):
        pltpu.make_async_copy(ref, ref, sem).wait()

    @pl.when(is_worker)
    def _():
        await_bytes(meta_in, recv_sem.at[0])
        block = lax.broadcasted_iota(I32, (8, 128), 1) // 32
        for f in range(16):
            turned = jnp.zeros((8, 128), F32)
            for q in range(4):
                source = meta_in[8 * q : 8 * q + 8, 0, f // 4 * 128 : f // 4 * 128 + 128]
                shift_by = (q - f % 4) % 4 * 32
                turned = jnp.where(block == q, pltpu.roll(source, shift_by, 1) if shift_by else source, turned)
            meta_turn[f] = turned
        meta = jnp.concatenate([meta_turn[:, group, :] for group in range(8)], axis=1)
        position = meta[14:15] * 32.0 + meta[15:16] - 1.0
        part_row = lax.broadcasted_iota(I32, (16, 1024), 0)
        right = jnp.where(part_row < 11, meta, jnp.where(part_row < 14, 1.0, 0.0)).astype(BF)
        shift = jnp.concatenate([meta[13:16], meta[0:13]], axis=0)
        raised = jnp.where(
            part_row < 8, -2.0 * meta, jnp.where((part_row >= 11) & (part_row < 14), shift, 0.0)
        )
        raised = jnp.where(part_row == 14, meta[11:12], raised).astype(BF)
        factor = jnp.where(part_row == 14, meta[13:14], jnp.where(part_row == 15, meta[12:13], 0.0)).astype(BF)

        for chunk in range(8):
            line = lax.broadcasted_iota(I32, (64, 1), 0) + 64 * (chunk % 4)
            half = 1 - core if chunk < 4 else core
            order = line // 32 * 64 + half * 32 + line % 32
            hit = (position == order.astype(F32)).astype(BF)
            pick[pl.ds(64 * chunk, 64), :] = hit
        picked = lax.dot_general(pick[...], raised, (((1,), (1,)), ((), ())), preferred_element_type=F32)
        lift[0:256, 0:16] = picked[256:512].astype(BF)
        lift[256:512, 0:16] = picked[0:256].astype(BF)
        swap = pltpu.make_async_remote_copy(
            src_ref=lift, dst_ref=lift_in, send_sem=pair_sem.at[0], recv_sem=pair_sem.at[1],
            device_id=peer, device_id_type=MESH,
        )
        swap.start()
        swap.wait_recv()
        spread = lax.broadcasted_iota(I32, (512, 16), 1)
        ones = ((spread >= 8) & (spread < 11)) | (spread == 15)
        left = picked + lift_in[:, 0:16].astype(F32) + jnp.where(ones, 1.0, 0.0)
        left = left.astype(BF)
        scale = -kernel_rate * math.log2(math.e)

        def form(chunk):
            rows = slice(64 * chunk, 64 * chunk + 64)
            distance = jnp.dot(left[rows], right, preferred_element_type=F32)
            coef = jnp.dot(left[rows], factor, preferred_element_type=F32)
            diagonal = pick[rows, :].astype(F32)
            entry = (jnp.exp2(distance * scale) + diagonal).astype(BF)
            mat[rows, :] = entry * coef.astype(BF)

        left_lanes = lax.broadcasted_iota(I32, (8, 16, 128), 2) < 64

        def combine(first):
            rows = slice(first, first + 256)
            data = data_in[...].reshape(1024, 128)
            chosen = jnp.dot(pick[rows], data, preferred_element_type=F32).reshape(8, 32, 128)
            product = jnp.dot(mat[rows], data, preferred_element_type=F32).reshape(8, 32, 128)
            above = pltpu.roll(chosen[:, 0:16], 64, 2) - product[:, 0:16]
            below = chosen[:, 16:32] - pltpu.roll(product[:, 16:32], 64, 2)
            return jnp.where(left_lanes, above, below)

        for chunk in range(4):
            form(chunk)
        await_bytes(data_in, recv_sem.at[1])
        part[...] = combine(0)
        trade = pltpu.make_async_remote_copy(
            src_ref=part, dst_ref=part_in,
            send_sem=pair_sem.at[2], recv_sem=pair_sem.at[3], device_id=peer, device_id_type=MESH,
        )
        trade.start()
        for chunk in range(4, 8):
            form(chunk)
        mine_rows = combine(256)
        trade.wait_recv()
        last_rank = rank_s[2, leaf]
        mine_rows = mine_rows + part_in[...]
        order = (
            lax.broadcasted_iota(I32, (8, 16, 128), 0) * 64 + core * 32
            + jnp.where(left_lanes, 0, 16) + lax.broadcasted_iota(I32, (8, 16, 128), 1)
        )
        blocks[...] = jnp.where(order < last_rank, mine_rows, 0.0).astype(BF)

        for number in OUT_ORDER:
            block = blocks.at[number // 2 % 4 * 2 + number % 2]

            @pl.when(chip != number)
            def _():
                pltpu.make_async_remote_copy(
                    src_ref=block,
                    dst_ref=pieces.at[slot],
                    send_sem=send_sem.at[2],
                    recv_sem=recv_sem.at[2],
                    device_id=device(number),
                    device_id_type=MESH,
                ).start()

        pltpu.make_async_copy(blocks.at[x * 2 + y], pieces.at[slot], recv_sem.at[2]).start()

    await_bytes(pieces, recv_sem.at[2])
    left_part = lax.broadcasted_iota(I32, (16, 128), 1) < 64
    for v in range(8):
        even = pieces[2 * v].astype(F32)
        odd = pieces[2 * v + 1].astype(F32)
        columns = slice(128 * v, 128 * v + 128)
        out[0, 0:16, columns] = jnp.where(left_part, even, pltpu.roll(odd, 64, 1)).astype(BF)
        out[0, 16:32, columns] = jnp.where(left_part, pltpu.roll(even, 64, 1), odd).astype(BF)

    @pl.when(is_worker)
    def _():
        pltpu.make_async_copy(lift, lift_in, pair_sem.at[0]).wait()
        pltpu.make_async_copy(part, part_in, pair_sem.at[2]).wait()
        await_bytes(data_in.at[pl.ds(0, 31), pl.ds(0, 16)], send_sem.at[2])
        await_bytes(meta_in.at[pl.ds(0, 15)], send_sem.at[0])
        await_bytes(data_in.at[pl.ds(0, 15)], send_sem.at[1])

    @pl.when(jnp.logical_not(is_worker))
    def _():
        await_bytes(meta_in.at[pl.ds(0, 16)], send_sem.at[0])
        await_bytes(data_in.at[pl.ds(0, 16)], send_sem.at[1])


def body(samples, omega, points, ranks, pivots):
    anywhere = pl.BlockSpec(memory_space=pl.ANY)
    return pl.pallas_call(
        kernel,
        out_shape=pltpu.VMEM((1, 32, 1024), BF),
        in_specs=[anywhere] * 5,
        out_specs=pl.BlockSpec(memory_space=pltpu.VMEM),
        scratch_shapes=[
            pltpu.VMEM((8, 32), BF),
            pltpu.VMEM((2, 1, 512), I32),
            pltpu.SMEM((3, 32), I32),
            pltpu.VMEM((32, 1024), BF),
            pltpu.VMEM((32, 1024), BF),
            pltpu.VMEM((16, 32, 128), BF),
            pltpu.VMEM((1, 512), F32),
            pltpu.VMEM((32, 1, 512), F32),
            pltpu.VMEM((16, 8, 128), F32),
            pltpu.VMEM((32, 32, 128), BF),
            pltpu.VMEM((512, 1024), BF),
            pltpu.VMEM((512, 1024), BF),
            pltpu.VMEM((512, 128), BF),
            pltpu.VMEM((512, 128), BF),
            pltpu.VMEM((8, 16, 128), F32),
            pltpu.VMEM((8, 16, 128), F32),
            pltpu.VMEM((8, 16, 128), BF),
            pltpu.VMEM((16, 16, 128), BF),
            pltpu.SemaphoreType.DMA((5,)),
            pltpu.SemaphoreType.DMA((3,)),
            pltpu.SemaphoreType.DMA((3,)),
            pltpu.SemaphoreType.DMA((4,)),
        ],
        compiler_params=pltpu.CompilerParams(
            collective_id=0, has_side_effects=True, vmem_limit_bytes=60 * 2**20
        ),
        cost_estimate=pl.CostEstimate(flops=300_000_000, bytes_accessed=200_000, transcendentals=524288),
    )(samples, omega, points[:, 0, :], ranks, pivots)


def solution(mesh):
    return jax.shard_map(
        body,
        mesh=mesh,
        in_specs=(
            P("leaf", "grid", None),
            P("leaf", "grid", None),
            P(None, "leaf", "grid"),
            P(),
            P(None, "leaf", None),
        ),
        out_specs=P("leaf", "grid", None),
        check_vma=False,
    )
```

time: 26.6 us -> 23.4 us (0.88)
  the two profiles are of different devices: /device:TPU:256 before, /device:TPU:1 now
where the time goes in v3:
time: 23.4 us; the launch traced here: 23.2 us
  Pallas kernels  22.6 us (97%)
  local copies, waits for them, and re-layouts  0.63 us (3%)
    pallas_call x1, Pallas kernels, body(): pl.pallas_call(kernel, out_shape=pltpu.VMEM((1, 32, 1024), BF), in_specs=...  22.6 us
    unnamed x1, local copies, waits for them, and re-layouts  0.63 us

profile of v3, /device:TPU:1, one launch (start us, length us, event | category | flops | bytes accessed | tf_op | source)
XLA Modules:
  0.0 23.2 jit_solution(4022749277781785937)
XLA Ops:
  0.0 22.6 %shard_map.55 = bf16[1,32,1024]{2,1,0:T(8,128)(2,1)S(1)} custom-call(bf16[1,32,1024]{2,1,0:T(8,128)(2,1)} %samples.1, bf16[1,32,1024]{2,1,0:T(8,128)(2,1)} %omega.1, bf16[8,32]{1,0:T(8,128)(2,1)} %bitcast.1, s32[3,32]{1,0:T(4,128)} %ranks.1, s32[2,1,512]{2,1,0:T(1,128)} %pivots.1), custom_call_target="tpu_custom_call" | custom-call | flops 300000000 | bytes 200000 | tf_op jit(solution)/shard_map/pallas_call | solution.py:289
  22.6 0.6 %copy.7 = bf16[1,32,1024]{2,1,0:T(8,128)(2,1)} copy(bf16[1,32,1024]{2,1,0:T(8,128)(2,1)S(1)} %shard_map.55) | data formatting | bytes 131072

commit v4 on v3

--- a/solution.py
+++ b/solution.py
@@ -14,11 +14,11 @@
 I32 = jnp.int32
 kernel_rate = 0.6
 
-NEAR = [z * 8 + x * 2 + y for y, z in [(0, 0), (0, 1), (0, 2), (1, 0)] for x in (0, 1, 3, 2)]
-MIDDLE = [p * 8 + c for p in (0, 1) for c in range(8)]
-PLANES = [1, 2, 0, 3]
+NEAR = [3, 7, 4, 2, 1, 6, 10, 14, 9, 13, 8, 16, 19, 22, 20, 17]
+MIDDLE = [p * 8 + c for p in (0, 3) for c in range(8)]
+PLANES = [1, 3, 0, 2]
 FAR_FIRST = sorted(range(32), key=lambda c: -(c // 8 * 10 + min(c // 2 % 4, 4 - c // 2 % 4) * 2 + c % 2))
-OUT_ORDER = [p * 8 + c for c in [0, 2, 6, 1, 4, 3, 7, 5] for p in [0, 3, 2, 1]]
+OUT_ORDER = [[p * 8 + c for p in range(4) for c in cs] for cs in ((0, 2, 1, 3), (6, 4, 7, 5))]
 
 
 def total(flags):
@@ -59,20 +59,22 @@
     peer = (leaf, grid + 1 - 2 * core)
 
     loads = [
-        pltpu.make_async_copy(omega.at[0], om_v, local_sem.at[3]),
-        pltpu.make_async_copy(samples.at[0], sa_v, local_sem.at[4]),
         pltpu.make_async_copy(points, pts_v, local_sem.at[0]),
         pltpu.make_async_copy(pivots, piv_v, local_sem.at[1]),
         pltpu.make_async_copy(ranks, rank_s, local_sem.at[2]),
     ]
-    for load in loads:
+    bulk = [
+        pltpu.make_async_copy(omega.at[0], om_v, local_sem.at[3]),
+        pltpu.make_async_copy(samples.at[0], sa_v, local_sem.at[4]),
+    ]
+    for load in loads + bulk:
         load.start()
 
     barrier = pltpu.get_barrier_semaphore()
 
     @pl.when(is_worker)
     def _():
-        for number in FAR_FIRST:
+        for number in FAR_FIRST[::-1]:
 
             @pl.when(chip != number)
             def _():
@@ -125,20 +127,12 @@
     at_field = lax.broadcasted_iota(I32, (16, 128), 0)
     at_block = lax.broadcasted_iota(I32, (16, 128), 1) // 32
     for part_of in range(4):
-        chosen_row = jnp.where(at_field == 4 * part_of + at_block, tile, 0.0)
+        chosen_row = jnp.where(at_field == 4 * part_of + (at_block + 4 - chip % 4) % 4, tile, 0.0)
         meta_out[:, 128 * part_of : 128 * part_of + 128] = jnp.sum(chosen_row, axis=0, keepdims=True)
 
-    left_half = lax.broadcasted_iota(I32, (32, 128), 1) < 64
-    for v in range(8):
-        o = om_v[:, 128 * v : 128 * v + 128].astype(F32)
-        a = sa_v[:, 128 * v : 128 * v + 128].astype(F32)
-        packed[2 * v] = jnp.where(left_half, o, pltpu.roll(a, 64, 1)).astype(BF)
-        packed[2 * v + 1] = jnp.where(left_half, pltpu.roll(o, 64, 1), a).astype(BF)
-
     @pl.when(is_worker)
     def _():
         pltpu.make_async_copy(meta_out, meta_in.at[meta_slot], recv_sem.at[0]).start()
-        pltpu.make_async_copy(packed.at[slot], data_in.at[chip], recv_sem.at[1]).start()
 
     pl.semaphore_wait(barrier, 16)
 
@@ -157,6 +151,20 @@
                 ).start()
 
     send_all(lambda w: meta_out, meta_in.at[meta_slot], 0)
+    for load in bulk:
+        load.wait()
+
+    left_half = lax.broadcasted_iota(I32, (32, 128), 1) < 64
+    for v in range(8):
+        o = om_v[:, 128 * v : 128 * v + 128].astype(F32)
+        a = sa_v[:, 128 * v : 128 * v + 128].astype(F32)
+        packed[2 * v] = jnp.where(left_half, o, pltpu.roll(a, 64, 1)).astype(BF)
+        packed[2 * v + 1] = jnp.where(left_half, pltpu.roll(o, 64, 1), a).astype(BF)
+
+    @pl.when(is_worker)
+    def _():
+        pltpu.make_async_copy(packed.at[slot], data_in.at[chip], recv_sem.at[1]).start()
+
     send_all(lambda w: packed.at[w], data_in.at[chip], 1)
 
     def await_bytes(ref, sem):
@@ -167,11 +175,11 @@
         await_bytes(meta_in, recv_sem.at[0])
         block = lax.broadcasted_iota(I32, (8, 128), 1) // 32
         for f in range(16):
-            turned = jnp.zeros((8, 128), F32)
-            for q in range(4):
+            turned = meta_in[0:8, 0, f // 4 * 128 : f // 4 * 128 + 128]
+            for q in range(1, 4):
                 source = meta_in[8 * q : 8 * q + 8, 0, f // 4 * 128 : f // 4 * 128 + 128]
-                shift_by = (q - f % 4) % 4 * 32
-                turned = jnp.where(block == q, pltpu.roll(source, shift_by, 1) if shift_by else source, turned)
+                turned = jnp.where(block == (q + f % 4) % 4, source, turned)
+            turned = pltpu.roll(turned, (4 - f % 4) * 32, 1) if f % 4 else turned
             meta_turn[f] = turned
         meta = jnp.concatenate([meta_turn[:, group, :] for group in range(8)], axis=1)
         position = meta[14:15] * 32.0 + meta[15:16] - 1.0
@@ -190,74 +198,82 @@
             order = line // 32 * 64 + half * 32 + line % 32
             hit = (position == order.astype(F32)).astype(BF)
             pick[pl.ds(64 * chunk, 64), :] = hit
-        picked = lax.dot_general(pick[...], raised, (((1,), (1,)), ((), ())), preferred_element_type=F32)
-        lift[0:256, 0:16] = picked[256:512].astype(BF)
-        lift[256:512, 0:16] = picked[0:256].astype(BF)
+        eight = jnp.concatenate([raised] * 8, axis=0)
+        picked = lax.dot_general(pick[...], eight, (((1,), (1,)), ((), ())), preferred_element_type=F32)
+        chunk_lane = lax.broadcasted_iota(I32, (64, 128), 1) // 16
+        gathered = total([jnp.where(chunk_lane == g, picked[64 * g : 64 * g + 64], 0.0) for g in range(8)])
+        lift[...] = pltpu.roll(gathered, 64, 1).astype(BF)
         swap = pltpu.make_async_remote_copy(
             src_ref=lift, dst_ref=lift_in, send_sem=pair_sem.at[0], recv_sem=pair_sem.at[1],
             device_id=peer, device_id_type=MESH,
         )
         swap.start()
+        right = jnp.concatenate([right] * 8, axis=0)
+        factor = jnp.concatenate([factor] * 8, axis=0)
         swap.wait_recv()
-        spread = lax.broadcasted_iota(I32, (512, 16), 1)
+        spread = lax.broadcasted_iota(I32, (64, 128), 1) % 16
         ones = ((spread >= 8) & (spread < 11)) | (spread == 15)
-        left = picked + lift_in[:, 0:16].astype(F32) + jnp.where(ones, 1.0, 0.0)
-        left = left.astype(BF)
+        left = gathered + lift_in[...].astype(F32) + jnp.where(ones, 1.0, 0.0)
         scale = -kernel_rate * math.log2(math.e)
 
         def form(chunk):
             rows = slice(64 * chunk, 64 * chunk + 64)
-            distance = jnp.dot(left[rows], right, preferred_element_type=F32)
-            coef = jnp.dot(left[rows], factor, preferred_element_type=F32)
+            one = jnp.where(chunk_lane == chunk, left, 0.0).astype(BF)
+            distance = jnp.dot(one, right, preferred_element_type=F32)
+            coef = jnp.dot(one, factor, preferred_element_type=F32)
             diagonal = pick[rows, :].astype(F32)
             entry = (jnp.exp2(distance * scale) + diagonal).astype(BF)
             mat[rows, :] = entry * coef.astype(BF)
 
         left_lanes = lax.broadcasted_iota(I32, (8, 16, 128), 2) < 64
 
-        def combine(first):
-            rows = slice(first, first + 256)
+        def combine(first, count):
+            rows = slice(first, first + 32 * count)
             data = data_in[...].reshape(1024, 128)
-            chosen = jnp.dot(pick[rows], data, preferred_element_type=F32).reshape(8, 32, 128)
-            product = jnp.dot(mat[rows], data, preferred_element_type=F32).reshape(8, 32, 128)
+            chosen = jnp.dot(pick[rows], data, preferred_element_type=F32).reshape(count, 32, 128)
+            product = jnp.dot(mat[rows], data, preferred_element_type=F32).reshape(count, 32, 128)
             above = pltpu.roll(chosen[:, 0:16], 64, 2) - product[:, 0:16]
             below = chosen[:, 16:32] - pltpu.roll(product[:, 16:32], 64, 2)
-            return jnp.where(left_lanes, above, below)
+            return jnp.where(left_lanes[0:count], above, below)
 
         for chunk in range(4):
             form(chunk)
         await_bytes(data_in, recv_sem.at[1])
-        part[...] = combine(0)
-        trade = pltpu.make_async_remote_copy(
-            src_ref=part, dst_ref=part_in,
-            send_sem=pair_sem.at[2], recv_sem=pair_sem.at[3], device_id=peer, device_id_type=MESH,
-        )
-        trade.start()
+        trades = []
+        for k in range(2):
+            part[4 * k : 4 * k + 4] = combine(128 * k, 4)
+            trade = pltpu.make_async_remote_copy(
+                src_ref=part.at[pl.ds(4 * k, 4)], dst_ref=part_in.at[pl.ds(4 * k, 4)],
+                send_sem=pair_sem.at[2 + 2 * k], recv_sem=pair_sem.at[3 + 2 * k],
+                device_id=peer, device_id_type=MESH,
+            )
+            trade.start()
+            trades.append(trade)
         for chunk in range(4, 8):
             form(chunk)
-        mine_rows = combine(256)
-        trade.wait_recv()
+        mine_rows = combine(256, 8)
         last_rank = rank_s[2, leaf]
-        mine_rows = mine_rows + part_in[...]
         order = (
             lax.broadcasted_iota(I32, (8, 16, 128), 0) * 64 + core * 32
             + jnp.where(left_lanes, 0, 16) + lax.broadcasted_iota(I32, (8, 16, 128), 1)
         )
-        blocks[...] = jnp.where(order < last_rank, mine_rows, 0.0).astype(BF)
-
-        for number in OUT_ORDER:
-            block = blocks.at[number // 2 % 4 * 2 + number % 2]
-
-            @pl.when(chip != number)
-            def _():
-                pltpu.make_async_remote_copy(
-                    src_ref=block,
-                    dst_ref=pieces.at[slot],
-                    send_sem=send_sem.at[2],
-                    recv_sem=recv_sem.at[2],
-                    device_id=device(number),
-                    device_id_type=MESH,
-                ).start()
+        for k in range(2):
+            trades[k].wait_recv()
+            these = slice(4 * k, 4 * k + 4)
+            blocks[these] = jnp.where(order[these] < last_rank, mine_rows[these] + part_in[these], 0.0).astype(BF)
+            for number in OUT_ORDER[k]:
+                block = blocks.at[number % 8]
+
+                @pl.when(chip != number)
+                def _():
+                    pltpu.make_async_remote_copy(
+                        src_ref=block,
+                        dst_ref=pieces.at[slot],
+                        send_sem=send_sem.at[2],
+                        recv_sem=recv_sem.at[2],
+                        device_id=device(number),
+                        device_id_type=MESH,
+                    ).start()
 
         pltpu.make_async_copy(blocks.at[x * 2 + y], pieces.at[slot], recv_sem.at[2]).start()
 
@@ -273,7 +289,8 @@
     @pl.when(is_worker)
     def _():
         pltpu.make_async_copy(lift, lift_in, pair_sem.at[0]).wait()
-        pltpu.make_async_copy(part, part_in, pair_sem.at[2]).wait()
+        for k in range(2):
+            pltpu.make_async_copy(part.at[pl.ds(4 * k, 4)], part_in.at[pl.ds(4 * k, 4)], pair_sem.at[2 + 2 * k]).wait()
         await_bytes(data_in.at[pl.ds(0, 31), pl.ds(0, 16)], send_sem.at[2])
         await_bytes(meta_in.at[pl.ds(0, 15)], send_sem.at[0])
         await_bytes(data_in.at[pl.ds(0, 15)], send_sem.at[1])
@@ -304,8 +321,8 @@
             pltpu.VMEM((32, 32, 128), BF),
             pltpu.VMEM((512, 1024), BF),
             pltpu.VMEM((512, 1024), BF),
-            pltpu.VMEM((512, 128), BF),
-            pltpu.VMEM((512, 128), BF),
+            pltpu.VMEM((64, 128), BF),
+            pltpu.VMEM((64, 128), BF),
             pltpu.VMEM((8, 16, 128), F32),
             pltpu.VMEM((8, 16, 128), F32),
             pltpu.VMEM((8, 16, 128), BF),
@@ -313,7 +330,7 @@
             pltpu.SemaphoreType.DMA((5,)),
             pltpu.SemaphoreType.DMA((3,)),
             pltpu.SemaphoreType.DMA((3,)),
-            pltpu.SemaphoreType.DMA((4,)),
+            pltpu.SemaphoreType.DMA((6,)),
         ],
         compiler_params=pltpu.CompilerParams(
             collective_id=0, has_side_effects=True, vmem_limit_bytes=60 * 2**20

time: 23.4 us -> 21.9 us (0.936)
  Pallas kernels: 22.6 us -> 21.1 us
    pallas_call x1, Pallas kernels: 22.6 us -> 21.1 us  [body(): pl.pallas_call(kernel, out_shape=pltpu.VMEM((1, 32, 1024), BF), in_specs=...]
where the time goes in v4:
time: 21.9 us; the launch traced here: 21.7 us
  Pallas kernels  21.1 us (96%)
  local copies, waits for them, and re-layouts  0.63 us (3%)
    pallas_call x1, Pallas kernels, body(): pl.pallas_call(kernel, out_shape=pltpu.VMEM((1, 32, 1024), BF), in_specs=...  21.1 us
    unnamed x1, local copies, waits for them, and re-layouts  0.63 us

profile of v4, /device:TPU:1, one launch (start us, length us, event | category | flops | bytes accessed | tf_op | source)
XLA Modules:
  0.0 21.7 jit_solution(3293519598956994049)
XLA Ops:
  0.0 21.1 %shard_map.55 = bf16[1,32,1024]{2,1,0:T(8,128)(2,1)S(1)} custom-call(bf16[1,32,1024]{2,1,0:T(8,128)(2,1)} %samples.1, bf16[1,32,1024]{2,1,0:T(8,128)(2,1)} %omega.1, bf16[8,32]{1,0:T(8,128)(2,1)} %bitcast.1, s32[3,32]{1,0:T(4,128)} %ranks.1, s32[2,1,512]{2,1,0:T(1,128)} %pivots.1), custom_call_target="tpu_custom_call" | custom-call | flops 300000000 | bytes 200000 | tf_op jit(solution)/shard_map/pallas_call | solution.py:306
  21.1 0.6 %copy.7 = bf16[1,32,1024]{2,1,0:T(8,128)(2,1)} copy(bf16[1,32,1024]{2,1,0:T(8,128)(2,1)S(1)} %shard_map.55) | data formatting | bytes 131072

commit v5 on v4

--- a/solution.py
+++ b/solution.py
@@ -136,8 +136,8 @@
 
     pl.semaphore_wait(barrier, 16)
 
-    def send_all(source, target, number):
-        for w in range(16):
+    def send_all(source, target, number, order=tuple(range(16))):
+        for w in order:
 
             @pl.when(chip != worker_chips[w])
             def _():
@@ -165,7 +165,13 @@
     def _():
         pltpu.make_async_copy(packed.at[slot], data_in.at[chip], recv_sem.at[1]).start()
 
-    send_all(lambda w: packed.at[w], data_in.at[chip], 1)
+    @pl.when(chip % 2 == 0)
+    def _():
+        send_all(lambda w: packed.at[w], data_in.at[chip], 1)
+
+    @pl.when(chip % 2 == 1)
+    def _():
+        send_all(lambda w: packed.at[w], data_in.at[chip], 1, tuple(range(8, 16)) + tuple(range(8)))
 
     def await_bytes(ref, sem):
         pltpu.make_async_copy(ref, ref, sem).wait()
@@ -192,31 +198,42 @@
         raised = jnp.where(part_row == 14, meta[11:12], raised).astype(BF)
         factor = jnp.where(part_row == 14, meta[13:14], jnp.where(part_row == 15, meta[12:13], 0.0)).astype(BF)
 
-        for chunk in range(8):
-            line = lax.broadcasted_iota(I32, (64, 1), 0) + 64 * (chunk % 4)
-            half = 1 - core if chunk < 4 else core
-            order = line // 32 * 64 + half * 32 + line % 32
-            hit = (position == order.astype(F32)).astype(BF)
-            pick[pl.ds(64 * chunk, 64), :] = hit
         eight = jnp.concatenate([raised] * 8, axis=0)
-        picked = lax.dot_general(pick[...], eight, (((1,), (1,)), ((), ())), preferred_element_type=F32)
         chunk_lane = lax.broadcasted_iota(I32, (64, 128), 1) // 16
-        gathered = total([jnp.where(chunk_lane == g, picked[64 * g : 64 * g + 64], 0.0) for g in range(8)])
-        lift[...] = pltpu.roll(gathered, 64, 1).astype(BF)
-        swap = pltpu.make_async_remote_copy(
-            src_ref=lift, dst_ref=lift_in, send_sem=pair_sem.at[0], recv_sem=pair_sem.at[1],
-            device_id=peer, device_id_type=MESH,
-        )
-        swap.start()
+        gathered = [None, None]
+        swaps = [None, None]
+        for k in (1, 0):
+            half = core if k else 1 - core
+            for chunk in range(4 * k, 4 * k + 4):
+                line = lax.broadcasted_iota(I32, (64, 1), 0) + 64 * (chunk % 4)
+                order = line // 32 * 64 + half * 32 + line % 32
+                hit = (position == order.astype(F32)).astype(BF)
+                pick[pl.ds(64 * chunk, 64), :] = hit
+            picked = lax.dot_general(
+                pick[256 * k : 256 * k + 256], eight, (((1,), (1,)), ((), ())), preferred_element_type=F32
+            )
+            gathered[k] = total(
+                [jnp.where(chunk_lane == 4 * k + g, picked[64 * g : 64 * g + 64], 0.0) for g in range(4)]
+            )
+            lift[1 - k] = pltpu.roll(gathered[k], 64, 1).astype(BF)
+            swaps[1 - k] = pltpu.make_async_remote_copy(
+                src_ref=lift.at[1 - k], dst_ref=lift_in.at[1 - k],
+                send_sem=pair_sem.at[6 - 6 * k], recv_sem=pair_sem.at[7 - 6 * k],
+                device_id=peer, device_id_type=MESH,
+            )
+            swaps[1 - k].start()
         right = jnp.concatenate([right] * 8, axis=0)
         factor = jnp.concatenate([factor] * 8, axis=0)
-        swap.wait_recv()
         spread = lax.broadcasted_iota(I32, (64, 128), 1) % 16
-        ones = ((spread >= 8) & (spread < 11)) | (spread == 15)
-        left = gathered + lift_in[...].astype(F32) + jnp.where(ones, 1.0, 0.0)
+        ones = jnp.where(((spread >= 8) & (spread < 11)) | (spread == 15), 1.0, 0.0)
+
+        def selected(k):
+            swaps[k].wait_recv()
+            return gathered[k] + lift_in[k].astype(F32) + ones
+
         scale = -kernel_rate * math.log2(math.e)
 
-        def form(chunk):
+        def form(chunk, left):
             rows = slice(64 * chunk, 64 * chunk + 64)
             one = jnp.where(chunk_lane == chunk, left, 0.0).astype(BF)
             distance = jnp.dot(one, right, preferred_element_type=F32)
@@ -236,8 +253,9 @@
             below = chosen[:, 16:32] - pltpu.roll(product[:, 16:32], 64, 2)
             return jnp.where(left_lanes[0:count], above, below)
 
+        left = selected(0)
         for chunk in range(4):
-            form(chunk)
+            form(chunk, left)
         await_bytes(data_in, recv_sem.at[1])
         trades = []
         for k in range(2):
@@ -249,8 +267,9 @@
             )
             trade.start()
             trades.append(trade)
+        left = selected(1)
         for chunk in range(4, 8):
-            form(chunk)
+            form(chunk, left)
         mine_rows = combine(256, 8)
         last_rank = rank_s[2, leaf]
         order = (
@@ -288,7 +307,8 @@
 
     @pl.when(is_worker)
     def _():
-        pltpu.make_async_copy(lift, lift_in, pair_sem.at[0]).wait()
+        for k in range(2):
+            pltpu.make_async_copy(lift.at[k], lift_in.at[k], pair_sem.at[6 * k]).wait()
         for k in range(2):
             pltpu.make_async_copy(part.at[pl.ds(4 * k, 4)], part_in.at[pl.ds(4 * k, 4)], pair_sem.at[2 + 2 * k]).wait()
         await_bytes(data_in.at[pl.ds(0, 31), pl.ds(0, 16)], send_sem.at[2])
@@ -321,8 +341,8 @@
             pltpu.VMEM((32, 32, 128), BF),
             pltpu.VMEM((512, 1024), BF),
             pltpu.VMEM((512, 1024), BF),
-            pltpu.VMEM((64, 128), BF),
-            pltpu.VMEM((64, 128), BF),
+            pltpu.VMEM((2, 64, 128), BF),
+            pltpu.VMEM((2, 64, 128), BF),
             pltpu.VMEM((8, 16, 128), F32),
             pltpu.VMEM((8, 16, 128), F32),
             pltpu.VMEM((8, 16, 128), BF),
@@ -330,7 +350,7 @@
             pltpu.SemaphoreType.DMA((5,)),
             pltpu.SemaphoreType.DMA((3,)),
             pltpu.SemaphoreType.DMA((3,)),
-            pltpu.SemaphoreType.DMA((6,)),
+            pltpu.SemaphoreType.DMA((8,)),
         ],
         compiler_params=pltpu.CompilerParams(
             collective_id=0, has_side_effects=True, vmem_limit_bytes=60 * 2**20

time: 21.9 us -> 21.8 us (level)
  no operation moved by 1% of the time
where the time goes in v5:
time: 21.8 us; the launch traced here: 21.7 us
  Pallas kernels  21 us (96%)
  local copies, waits for them, and re-layouts  0.63 us (3%)
    pallas_call x1, Pallas kernels, body(): pl.pallas_call(kernel, out_shape=pltpu.VMEM((1, 32, 1024), BF), in_specs=...  21 us
    unnamed x1, local copies, waits for them, and re-layouts  0.63 us

profile of v5, /device:TPU:1, one launch (start us, length us, event | category | flops | bytes accessed | tf_op | source)
XLA Modules:
  0.0 21.7 jit_solution(165240455780806361)
XLA Ops:
  0.0 21.0 %shard_map.55 = bf16[1,32,1024]{2,1,0:T(8,128)(2,1)S(1)} custom-call(bf16[1,32,1024]{2,1,0:T(8,128)(2,1)} %samples.1, bf16[1,32,1024]{2,1,0:T(8,128)(2,1)} %omega.1, bf16[8,32]{1,0:T(8,128)(2,1)} %bitcast.1, s32[3,32]{1,0:T(4,128)} %ranks.1, s32[2,1,512]{2,1,0:T(1,128)} %pivots.1), custom_call_target="tpu_custom_call" | custom-call | flops 300000000 | bytes 200000 | tf_op jit(solution)/shard_map/pallas_call | solution.py:326
  21.0 0.6 %copy.7 = bf16[1,32,1024]{2,1,0:T(8,128)(2,1)} copy(bf16[1,32,1024]{2,1,0:T(8,128)(2,1)S(1)} %shard_map.55) | data formatting | bytes 131072

commit v6 on v5

--- a/solution.py
+++ b/solution.py
@@ -289,16 +289,17 @@
                         src_ref=block,
                         dst_ref=pieces.at[slot],
                         send_sem=send_sem.at[2],
-                        recv_sem=recv_sem.at[2],
+                        recv_sem=recv_sem.at[2 + slot // 8],
                         device_id=device(number),
                         device_id_type=MESH,
                     ).start()
 
-        pltpu.make_async_copy(blocks.at[x * 2 + y], pieces.at[slot], recv_sem.at[2]).start()
-
-    await_bytes(pieces, recv_sem.at[2])
+        pltpu.make_async_copy(blocks.at[x * 2 + y], pieces.at[slot], recv_sem.at[2 + slot // 8]).start()
+
     left_part = lax.broadcasted_iota(I32, (16, 128), 1) < 64
     for v in range(8):
+        if v % 4 == 0:
+            await_bytes(pieces.at[pl.ds(2 * v, 8)], recv_sem.at[2 + v // 4])
         even = pieces[2 * v].astype(F32)
         odd = pieces[2 * v + 1].astype(F32)
         columns = slice(128 * v, 128 * v + 128)
@@ -349,7 +350,7 @@
             pltpu.VMEM((16, 16, 128), BF),
             pltpu.SemaphoreType.DMA((5,)),
             pltpu.SemaphoreType.DMA((3,)),
-            pltpu.SemaphoreType.DMA((3,)),
+            pltpu.SemaphoreType.DMA((4,)),
             pltpu.SemaphoreType.DMA((8,)),
         ],
         compiler_params=pltpu.CompilerParams(

time: 21.8 us -> 21.8 us (level)
  no operation moved by 1% of the time
where the time goes in v6:
time: 21.8 us; the launch traced here: 21.7 us
  Pallas kernels  21.1 us (97%)
  local copies, waits for them, and re-layouts  0.63 us (3%)
    pallas_call x1, Pallas kernels, body(): pl.pallas_call(kernel, out_shape=pltpu.VMEM((1, 32, 1024), BF), in_specs=...  21.1 us
    unnamed x1, local copies, waits for them, and re-layouts  0.63 us

profile of v6, /device:TPU:1, one launch (start us, length us, event | category | flops | bytes accessed | tf_op | source)
XLA Modules:
  0.0 21.7 jit_solution(17794915825894028747)
XLA Ops:
  0.0 21.1 %shard_map.55 = bf16[1,32,1024]{2,1,0:T(8,128)(2,1)S(1)} custom-call(bf16[1,32,1024]{2,1,0:T(8,128)(2,1)} %samples.1, bf16[1,32,1024]{2,1,0:T(8,128)(2,1)} %omega.1, bf16[8,32]{1,0:T(8,128)(2,1)} %bitcast.1, s32[3,32]{1,0:T(4,128)} %ranks.1, s32[2,1,512]{2,1,0:T(1,128)} %pivots.1), custom_call_target="tpu_custom_call" | custom-call | flops 300000000 | bytes 200000 | tf_op jit(solution)/shard_map/pallas_call | solution.py:327
  21.1 0.6 %copy.7 = bf16[1,32,1024]{2,1,0:T(8,128)(2,1)} copy(bf16[1,32,1024]{2,1,0:T(8,128)(2,1)S(1)} %shard_map.55) | data formatting | bytes 131072

commit v7 on v5

--- a/solution.py
+++ b/solution.py
@@ -165,13 +165,12 @@
     def _():
         pltpu.make_async_copy(packed.at[slot], data_in.at[chip], recv_sem.at[1]).start()
 
-    @pl.when(chip % 2 == 0)
-    def _():
-        send_all(lambda w: packed.at[w], data_in.at[chip], 1)
-
-    @pl.when(chip % 2 == 1)
-    def _():
-        send_all(lambda w: packed.at[w], data_in.at[chip], 1, tuple(range(8, 16)) + tuple(range(8)))
+    for turn in range(4):
+
+        @pl.when(x == turn)
+        def _():
+            turned = tuple((w + 4 * turn) % 16 for w in range(16))
+            send_all(lambda w: packed.at[w], data_in.at[chip], 1, turned)
 
     def await_bytes(ref, sem):
         pltpu.make_async_copy(ref, ref, sem).wait()

time: 21.8 us -> 21.7 us (level)
  no operation moved by 1% of the time
where the time goes in v7:
time: 21.7 us; the launch traced here: 21.5 us
  Pallas kernels  20.9 us (96%)
  local copies, waits for them, and re-layouts  0.63 us (3%)
    pallas_call x1, Pallas kernels, body(): pl.pallas_call(kernel, out_shape=pltpu.VMEM((1, 32, 1024), BF), in_specs=...  20.9 us
    unnamed x1, local copies, waits for them, and re-layouts  0.63 us

profile of v7, /device:TPU:1, one launch (start us, length us, event | category | flops | bytes accessed | tf_op | source)
XLA Modules:
  0.0 21.5 jit_solution(8611320486712101088)
XLA Ops:
  0.0 20.9 %shard_map.55 = bf16[1,32,1024]{2,1,0:T(8,128)(2,1)S(1)} custom-call(bf16[1,32,1024]{2,1,0:T(8,128)(2,1)} %samples.1, bf16[1,32,1024]{2,1,0:T(8,128)(2,1)} %omega.1, bf16[8,32]{1,0:T(8,128)(2,1)} %bitcast.1, s32[3,32]{1,0:T(4,128)} %ranks.1, s32[2,1,512]{2,1,0:T(1,128)} %pivots.1), custom_call_target="tpu_custom_call" | custom-call | flops 300000000 | bytes 200000 | tf_op jit(solution)/shard_map/pallas_call | solution.py:325
  20.9 0.6 %copy.7 = bf16[1,32,1024]{2,1,0:T(8,128)(2,1)} copy(bf16[1,32,1024]{2,1,0:T(8,128)(2,1)S(1)} %shard_map.55) | data formatting | bytes 131072
